TPU v7x, 32 devices: a whole 2x2x4 slice. The times are simulated.
32 devices in a mesh: groups: 2 (over y), var: 8 (over z, x), tm: 2 (over core).
Axes of the slice: x: 2, y: 2, z: 4, core: 2. Of those that a mesh axis runs over, the one named last changes fastest.
Arguments:
- series: bfloat16 [4, 512, 4096], P('groups', 'var', 'tm'), parts along dimension 0, may hold values from -71 to 71
- target: float32 [4, 512, 720], P('groups', 'var', 'tm'), parts along dimension 0, may hold values from -71 to 71
- w_embed: bfloat16 [4096, 512], P('tm'), may hold values from -0.09375 to 0.09375
- w_query: bfloat16 [512, 256], P(None, 'tm'), may hold values from -0.25 to 0.25
- w_key: bfloat16 [512, 256], P(None, 'tm'), may hold values from -0.25 to 0.25
- w_value: bfloat16 [512, 256], P(None, 'tm'), may hold values from -0.25 to 0.25
- w_out: bfloat16 [256, 512], P('tm'), may hold values from -0.375 to 0.375
- norm_gain: float32 [512], replicated, may hold values from 0.5 to 1.5
- w_head: bfloat16 [512, 720], P(None, 'tm'), may hold values from -0.25 to 0.25
Outputs:
- predicted_values: float32 [4, 512, 720], P('groups', 'var', 'tm'), parts along dimension 0
- question_projection_derivative: float32 [1024, 256], P('groups', 'tm'), parts along dimension 0
- final_projection_derivative: float32 [512, 512], P(('groups', 'tm')), parts along dimension 0
- layernorm_scale_derivative: float32 [1024], P('groups'), parts along dimension 0
- future_readout_derivative: float32 [1024, 720], P('groups', 'tm'), parts along dimension 0
There are 2 independent parts, one for each index of `groups`. A program takes and returns all parts, laid end to end along the dimension named above; an argument that names none is the same for every part. Nothing has to cross between parts.
All inputs are finite; a program needn't handle non-finite values.
Results may differ from a plain program's by a relative error of at most 0.015.
Values may be sent and summed in bfloat16 or wider, within the bound.
A program may use at most 128 MiB of HBM per device.

v0:
```python
import jax
import jax.numpy as jnp
from jax import lax
from jax.sharding import PartitionSpec as P

HEAD_DIM = 64
HOR = 720
SAMPLES = 2
epsilon = 1e-05


def split_heads(tensor_in):
    return tensor_in.reshape(tensor_in.shape[:-1] + (tensor_in.shape[-1] // HEAD_DIM, HEAD_DIM))


def project(inputs, matrix):
    return jnp.einsum("svd,da->sva", inputs, matrix, preferred_element_type=jnp.float32).astype(
        jnp.bfloat16
    )


def forward_attend(queries, key_rows, value_rows):
    scores = jnp.einsum(
        "nhe,mhe->hnm", queries, key_rows, preferred_element_type=jnp.float32
    ) * HEAD_DIM ** (-0.5)
    powers = jnp.exp(scores)
    row_sums = jnp.sum(powers, axis=2)
    summed = jnp.einsum(
        "hnm,mhe->nhe", powers.astype(jnp.bfloat16), value_rows, preferred_element_type=jnp.float32
    )
    return (summed / jnp.transpose(row_sums)[:, :, None], row_sums)


def attend_all(queries, key_rows, value_rows):
    contexts = []
    totals = []
    for sample in range(queries.shape[0]):
        context, row_sums = forward_attend(
            split_heads(queries[sample]),
            split_heads(key_rows[sample]),
            split_heads(value_rows[sample]),
        )
        contexts.append(context.reshape(queries.shape[1], queries.shape[2]))
        totals.append(row_sums)
    return (jnp.stack(contexts), totals)


def backward_attend(queries, key_rows, value_rows, row_sums, context, grad_context):
    scores = jnp.einsum(
        "nhe,mhe->hnm", queries, key_rows, preferred_element_type=jnp.float32
    ) * HEAD_DIM ** (-0.5)
    weights = jnp.exp(scores) / row_sums[:, :, None]
    grad_weights = jnp.einsum(
        "nhe,mhe->hnm",
        grad_context.astype(jnp.bfloat16),
        value_rows,
        preferred_element_type=jnp.float32,
    )
    row_dots = jnp.sum(grad_context * context, axis=2)
    grad_scores = (weights * (grad_weights - jnp.transpose(row_dots)[:, :, None])).astype(
        jnp.bfloat16
    )
    return jnp.einsum(
        "hnm,mhe->nhe", grad_scores, key_rows, preferred_element_type=jnp.float32
    ) * HEAD_DIM ** (-0.5)


def backward_all(queries, key_rows, value_rows, totals, context, grad_context):
    results = []
    for sample in range(queries.shape[0]):
        grad_rows = backward_attend(
            split_heads(queries[sample]),
            split_heads(key_rows[sample]),
            split_heads(value_rows[sample]),
            totals[sample],
            split_heads(context[sample]),
            split_heads(grad_context[sample]),
        )
        results.append(grad_rows.reshape(queries.shape[1], queries.shape[2]))
    return jnp.stack(results).astype(jnp.bfloat16)


def per_device(series, target, w_embed, w_query, w_key, w_value, w_out, norm_gain, w_head):
    samples, var_rows, steps_local = series.shape
    look_total = steps_local * lax.axis_size("tm")
    series_f = series.astype(jnp.float32)
    level_sum, square_sum = lax.psum(
        (jnp.sum(series_f, axis=2), jnp.sum(series_f * series_f, axis=2)), "tm"
    )
    instance_average = level_sum / look_total
    spread = square_sum / look_total - instance_average * instance_average
    centered = series_f - instance_average[:, :, None]
    instance_dispersion = jnp.sqrt(spread + epsilon)
    normed = (centered / instance_dispersion[:, :, None]).astype(jnp.bfloat16)
    partial_embed = jnp.einsum("svl,ld->svd", normed, w_embed, preferred_element_type=jnp.float32)
    hidden = lax.psum(partial_embed, "tm").astype(jnp.bfloat16)
    queries = project(hidden, w_query)
    key_rows = project(hidden, w_key)
    value_rows = project(hidden, w_value)
    all_keys, all_values = (
        lax.all_gather(key_rows, "var", axis=1, tiled=True),
        lax.all_gather(value_rows, "var", axis=1, tiled=True),
    )
    context, totals = attend_all(queries, all_keys, all_values)
    context_low = context.astype(jnp.bfloat16)
    mixing = lax.psum(
        jnp.einsum("sva,ad->svd", context_low, w_out, preferred_element_type=jnp.float32).astype(
            jnp.bfloat16
        ),
        "tm",
    ).astype(jnp.float32)
    residual = hidden.astype(jnp.float32) + mixing
    shifted = residual - jnp.mean(residual, axis=2, keepdims=True)
    norm_root = jnp.sqrt(jnp.mean(shifted * shifted, axis=2, keepdims=True) + epsilon)
    unit_rows = shifted / norm_root
    normal_out = (unit_rows * norm_gain).astype(jnp.bfloat16)
    future_rescaler = jnp.einsum(
        "svd,dh->svh", normal_out, w_head, preferred_element_type=jnp.float32
    )
    predicted_values = (
        future_rescaler * instance_dispersion[:, :, None] + instance_average[:, :, None]
    )
    errors = (
        future_rescaler - (target - instance_average[:, :, None]) / instance_dispersion[:, :, None]
    )
    grad_horizon = (errors * (2.0 / (SAMPLES * HOR))).astype(jnp.bfloat16)
    head_term = jnp.einsum(
        "svd,svh->dh", normal_out, grad_horizon, preferred_element_type=jnp.float32
    )
    grad_normal = lax.psum(
        jnp.einsum("svh,dh->svd", grad_horizon, w_head, preferred_element_type=jnp.float32).astype(
            jnp.bfloat16
        ),
        "tm",
    ).astype(jnp.float32)
    gain_term = jnp.sum(grad_normal * unit_rows, axis=(0, 1))
    grad_unit = grad_normal * norm_gain
    grad_mix = (
        (
            grad_unit
            - jnp.mean(grad_unit, axis=2, keepdims=True)
            - unit_rows * jnp.mean(grad_unit * unit_rows, axis=2, keepdims=True)
        )
        / norm_root
    ).astype(jnp.bfloat16)
    out_term = jnp.einsum("sva,svd->da", context_low, grad_mix, preferred_element_type=jnp.float32)
    grad_context = jnp.einsum("svd,ad->sva", grad_mix, w_out, preferred_element_type=jnp.float32)
    grad_query = backward_all(queries, all_keys, all_values, totals, context, grad_context)
    query_term = jnp.einsum("svd,sva->da", hidden, grad_query, preferred_element_type=jnp.float32)
    future_readout_derivative, gain_gradient_total, output_gradient_total, query_gradient_total = (
        lax.psum((head_term, gain_term, out_term, query_term), "var")
    )
    return (
        predicted_values,
        query_gradient_total,
        jnp.transpose(output_gradient_total),
        gain_gradient_total,
        future_readout_derivative,
    )


def solution(mesh):
    in_specs = (
        P("groups", "var", "tm"),
        P("groups", "var", "tm"),
        P("tm", None),
        P(None, "tm"),
        P(None, "tm"),
        P(None, "tm"),
        P("tm", None),
        P(),
        P(None, "tm"),
    )
    out_specs = (
        P("groups", "var", "tm"),
        P("groups", "tm"),
        P(("groups", "tm"), None),
        P("groups"),
        P("groups", "tm"),
    )
    return jax.shard_map(
        per_device, mesh=mesh, in_specs=in_specs, out_specs=out_specs, check_vma=False
    )
```

profile of v0, /device:TPU:0, one launch (start us, length us, event | category | flops | bytes accessed | tf_op | source)
XLA Modules:
  0.0 234.3 jit_solution(17725710917691183952)
XLA Ops:
  7.2 1.4 convert_reduce_fusion
  8.6 2.6 %all-reduce.1 = (f32[2,64]{1,0:T(2,128)S(1)}, f32[2,64]{1,0:T(2,128)S(1)}) all-reduce(f32[2,64]{1,0:T(2,128)S(1)} %get-tuple-element.6, f32[2,64]{1,0:T(2,128)S(1)} %get-tuple-element.5), channel_id=1, replica_groups=mesh['groups'=2,'var'=8,'tm'=2] {'tm'}, use_global_device_ids=true, to_apply=%region_3.0 | all-reduce | flops 256 | bytes 2048 | tf_op jit(solution)/shard_map/psum | solution.py:87
  11.8 1.6 fusion
  13.4 4.4 %all-reduce.12 = bf16[2,64,512]{2,1,0:T(8,128)(2,1)S(1)} all-reduce(f32[2,64,512]{2,1,0:T(8,128)S(1)} %fusion), channel_id=1, replica_groups=mesh['groups'=2,'var'=8,'tm'=2] {'tm'}, use_global_device_ids=true, to_apply=%region_4.0 | all-reduce | flops 65536 | bytes 393216 | tf_op jit(solution)/shard_map/psum | solution.py:96
  18.5 32.3 %all_gather.6 = bf16[2,512,128]{2,1,0:T(8,128)(2,1)S(1)} all-gather(bf16[2,64,128]{2,1,0:T(8,128)(2,1)S(1)} %convolution_convert_fusion.4), channel_id=1, replica_groups=mesh['groups'=2,'var'=8,'tm'=2] {'var'}, dimensions={1}, use_global_device_ids=true | all-gather | bytes 294912 | tf_op jit(solution)/shard_map/all_gather | solution.py:102
  51.1 30.7 %all_gather.7 = bf16[2,512,128]{2,1,0:T(8,128)(2,1)S(1)} all-gather(bf16[2,64,128]{2,1,0:T(8,128)(2,1)S(1)} %convolution_convert_fusion.2), channel_id=1, replica_groups=mesh['groups'=2,'var'=8,'tm'=2] {'var'}, dimensions={1}, use_global_device_ids=true | all-gather | bytes 294912 | tf_op jit(solution)/shard_map/all_gather | solution.py:101
  85.4 18.9 %all-reduce.7.cloned.1.call-done = bf16[2,64,512]{2,1,0:T(8,128)(2,1)} async-done(((bf16[2,64,512]{2,1,0:T(8,128)(2,1)}), bf16[2,64,512]{2,1,0:T(8,128)(2,1)}) %all-reduce.7.cloned.1.call-update) | async-done | bytes 131088 | tf_op jit(solution)/shard_map/psum | solution.py:106
  104.3 1.1 fusion.36
  105.4 1.1 multiply_reduce_fusion
  106.5 2.2 multiply_convert_fusion.1
  109.3 0.9 convolution_convert_fusion
  110.3 2.1 convolution_bitcast_fusion
  112.4 17.0 %all-reduce.9.cloned.1.call-done = bf16[2,64,512]{2,1,0:T(8,128)(2,1)} async-done(((bf16[2,64,512]{2,1,0:T(8,128)(2,1)}), bf16[2,64,512]{2,1,0:T(8,128)(2,1)}) %all-reduce.9.cloned.1.call-update) | async-done | bytes 131088 | tf_op jit(solution)/shard_map/psum | solution.py:130
  129.5 1.7 fusion.31
  131.2 1.1 fusion.34
  132.5 1.6 convolution_bitcast_fusion.1
  134.2 0.9 multiply_reduce_fusion.2
  135.1 1.1 fusion.15
  136.9 0.9 convolution_bitcast_fusion.2
  137.9 22.8 %psum.70 = f32[512]{0:T(512)} all-reduce(f32[512]{0:T(512)S(1)} %copy-done.12), channel_id=1, replica_groups=mesh['groups'=2,'var'=8,'tm'=2] {'var'}, use_global_device_ids=true, to_apply=%region_18.0 | all-reduce | flops 512 | bytes 4096 | tf_op jit(solution)/shard_map/psum | solution.py:151
  160.6 61.8 %all-reduce.11.cloned.1.call-done = (f32[512,128]{1,0:T(8,128)}, f32[128,512]{1,0:T(8,128)}, f32[512,360]{0,1:T(8,128)}) async-done(((f32[512,128]{1,0:T(8,128)}, f32[128,512]{1,0:T(8,128)}, f32[512,360]{0,1:T(8,128)}), (f32[512,128]{1,0:T(8,128)}, f32[128,512]{1,0:T(8,128)}, f32[512,360]{0,1:T(8,128)})) %all-reduce.11.cloned.1.call-update) | async-done | bytes 1261584 | tf_op jit(solution)/shard_map/psum | solution.py:151
  222.4 1.7 copy.55
  224.0 1.7 copy.56
  225.7 2.0 copy.57
  (73 shorter events, 6.7 us)
Async XLA Ops:
  7.2 4.6 %copy-start = (bf16[2048,512]{1,0:T(8,128)(2,1)S(1)}, bf16[2048,512]{1,0:T(8,128)(2,1)}, u32[]{:S(2)}) copy-start(bf16[2048,512]{1,0:T(8,128)(2,1)} %param.11) | copy-start | bytes 6291460
  7.2 97.1 %all-reduce.7.cloned.1.call-start = ((), (), s32[]{:S(2)}) async-start(), calls=%async_computation | async-start | bytes 262144 | tf_op jit(solution)/shard_map/psum | solution.py:106
  11.2 0.6 copy-start.16
  11.2 0.6 copy-start.17
  11.8 6.0 %copy-start.6 = (bf16[512,128]{1,0:T(8,128)(2,1)S(1)}, bf16[512,128]{1,0:T(8,128)(2,1)}, u32[]{:S(2)}) copy-start(bf16[512,128]{1,0:T(8,128)(2,1)} %param.13) | copy-start | bytes 393220
  11.8 6.2 %copy-start.7 = (bf16[512,128]{1,0:T(8,128)(2,1)S(1)}, bf16[512,128]{1,0:T(8,128)(2,1)}, u32[]{:S(2)}) copy-start(bf16[512,128]{1,0:T(8,128)(2,1)} %param.12) | copy-start | bytes 393220
  11.8 6.5 %copy-start.8 = (bf16[512,128]{1,0:T(8,128)(2,1)S(1)}, bf16[512,128]{1,0:T(8,128)(2,1)}, u32[]{:S(2)}) copy-start(bf16[512,128]{1,0:T(8,128)(2,1)} %param.14) | copy-start | bytes 393220
  50.8 33.6 %copy-start.2 = (bf16[128,512]{1,0:T(8,128)(2,1)S(1)}, bf16[128,512]{1,0:T(8,128)(2,1)}, u32[]{:S(2)}) copy-start(bf16[128,512]{1,0:T(8,128)(2,1)} %param.15) | copy-start | bytes 393220
  82.4 0.9 copy-start.13
  83.5 1.8 copy-start.15
  84.4 0.9 copy-start.5
  85.3 44.2 %all-reduce.9.cloned.1.call-start = ((), (), s32[]{:S(2)}) async-start(), calls=%async_computation.1 | async-start | bytes 262144 | tf_op jit(solution)/shard_map/psum | solution.py:130
  104.3 5.0 %copy-start.3 = (bf16[512,360]{0,1:T(8,128)(2,1)S(1)}, bf16[512,360]{0,1:T(8,128)(2,1)}, u32[]{:S(2)}) copy-start(bf16[512,360]{0,1:T(8,128)(2,1)} %param.17) | copy-start | bytes 1105924
  104.3 6.0 %copy-start.1 = (bf16[2,64,512]{2,1,0:T(8,128)(2,1)S(1)}, bf16[2,64,512]{2,1,0:T(8,128)(2,1)}, u32[]{:S(2)}) copy-start(bf16[2,64,512]{2,1,0:T(8,128)(2,1)} %all-reduce.7.cloned.1.call-done) | copy-start | bytes 393220
  105.4 1.1 copy-start.10
  106.5 2.2 copy-start.11
  108.7 0.6 copy-start.9
  110.2 112.1 %all-reduce.11.cloned.1.call-start = ((), (), s32[]{:S(2)}) async-start(), calls=%async_computation.2 | async-start | bytes 2523136 | tf_op jit(solution)/shard_map/psum | solution.py:151
  132.3 4.1 %copy-start.4 = (f32[64,2,64]{0,2,1:T(8,128)S(1)}, f32[64,2,64]{0,2,1:T(8,128)}, u32[]{:S(2)}) copy-start(f32[64,2,64]{0,2,1:T(8,128)} %get-tuple-element.30) | copy-start | bytes 98308
  132.3 4.1 %copy-start.14 = (f32[2,64]{1,0:T(2,128)S(1)}, f32[2,64]{1,0:T(2,128)}, u32[]{:S(2)}) copy-start(f32[2,64]{1,0:T(2,128)} %copy-done.13) | copy-start | bytes 1540
  135.1 2.8 %copy-start.12 = (f32[512]{0:T(512)S(1)}, f32[512]{0:T(512)}, u32[]{:S(2)}) copy-start(f32[512]{0:T(512)} %get-tuple-element.7) | copy-start | bytes 6148
Sparse Core Ops, SparseCore 0:
  85.4 18.8 all-reduce.6
  110.4 19.0 all-reduce.8
  138.0 84.3 all-reduce.10
where the time goes:
time: 235 us; the launch traced here: 234 us
  waiting for transfers between devices  97.8 us (42%)
  blocking collectives  92.8 us (39%)
  matrix products  14.4 us (6%)
  between operations  14.1 us (6%)
  local copies, waits for them, and re-layouts  7.82 us (3%)
  other arithmetic  7.29 us (3%)
    psum x1, waiting for transfers between devices, per_device(): lax.psum((head_term, gain_term, out_term, query_term), 'var')  61.8 us
    all_gather x1, blocking collectives, per_device(): lax.all_gather(value_rows, 'var', axis=1, tiled=True)  32.3 us
    all_gather x1, blocking collectives, per_device(): lax.all_gather(key_rows, 'var', axis=1, tiled=True)  30.7 us
    psum x1, blocking collectives, per_device(): lax.psum((head_term, gain_term, out_term, query_term), 'var')  22.8 us
    psum x1, waiting for transfers between devices, per_device(): lax.psum(jnp.einsum('sva,ad->svd', context_low, w_out, preferred_element_...  18.9 us
    psum x1, waiting for transfers between devices, per_device(): lax.psum(jnp.einsum('svh,dh->svd', grad_horizon, w_head, preferred_elemen...  17 us
    unnamed x39, local copies, waits for them, and re-layouts  6.63 us
  transfers between devices with their start and end apart: 3, of which 3 were waited for; matrix products, arithmetic and copies ran while one was open for 1% of the time, Pallas kernels for 0%

commit v1 on v0

--- a/solution.py
+++ b/solution.py
@@ -127,11 +127,14 @@
     head_term = jnp.einsum(
         "svd,svh->dh", normal_out, grad_horizon, preferred_element_type=jnp.float32
     )
-    grad_normal = lax.psum(
-        jnp.einsum("svh,dh->svd", grad_horizon, w_head, preferred_element_type=jnp.float32).astype(
-            jnp.bfloat16
+    grad_normal = jnp.sum(
+        lax.all_gather(
+            jnp.einsum(
+                "svh,dh->svd", grad_horizon, w_head, preferred_element_type=jnp.float32
+            ).astype(jnp.bfloat16),
+            "tm",
         ),
-        "tm",
+        axis=0,
     ).astype(jnp.float32)
     gain_term = jnp.sum(grad_normal * unit_rows, axis=(0, 1))
     grad_unit = grad_normal * norm_gain

time: 235 us -> 218 us (0.928)
  waiting for transfers between devices: 97.8 us -> 80.7 us
    psum x1 -> x0, waiting for transfers between devices: 17 us -> none  [per_device(): lax.psum(jnp.einsum('svh,dh->svd', grad_horizon, w_head, preferred_elemen...]
    unnamed x39 -> x49, local copies, waits for them, and re-layouts: 6.63 us -> 6.09 us
  transfers between devices with their start and end apart: 3 -> 2, of which waited for: 3 -> 2; matrix products, arithmetic and copies ran while one was open for 1% -> 0% of each run, Pallas kernels for 0% -> 0%
where the time goes in v1:
time: 218 us
  blocking collectives  94.9 us (44%)
  waiting for transfers between devices  80.7 us (37%)
  between operations  14.5 us (7%)
  matrix products  13.9 us (6%)
  local copies, waits for them, and re-layouts  7.29 us (3%)
  other arithmetic  6.4 us (3%)
    psum x1, waiting for transfers between devices, per_device(): lax.psum((head_term, gain_term, out_term, query_term), 'var')  61.8 us
    all_gather x1, blocking collectives, per_device(): lax.all_gather(value_rows, 'var', axis=1, tiled=True)  32.3 us
    all_gather x1, blocking collectives, per_device(): lax.all_gather(key_rows, 'var', axis=1, tiled=True)  30.9 us
    psum x1, blocking collectives, per_device(): lax.psum((head_term, gain_term, out_term, query_term), 'var')  22.7 us
    psum x1, waiting for transfers between devices, per_device(): lax.psum(jnp.einsum('sva,ad->svd', context_low, w_out, preferred_element_...  18.8 us
    unnamed x49, local copies, waits for them, and re-layouts  6.09 us
  transfers between devices with their start and end apart: 2, of which 2 were waited for; matrix products, arithmetic and copies ran while one was open for 0% of the time, Pallas kernels for 0%

profile of v1, /device:TPU:0, one launch (start us, length us, event | category | flops | bytes accessed | tf_op | source)
XLA Modules:
  0.0 217.7 jit_solution(7303542440859938488)
XLA Ops:
  7.2 1.4 convert_reduce_fusion
  8.6 2.6 %all-reduce.1 = (f32[2,64]{1,0:T(2,128)S(1)}, f32[2,64]{1,0:T(2,128)S(1)}) all-reduce(f32[2,64]{1,0:T(2,128)S(1)} %get-tuple-element.6, f32[2,64]{1,0:T(2,128)S(1)} %get-tuple-element.5), channel_id=1, replica_groups=mesh['groups'=2,'var'=8,'tm'=2] {'tm'}, use_global_device_ids=true, to_apply=%region_3.0 | all-reduce | flops 256 | bytes 2048 | tf_op jit(solution)/shard_map/psum | solution.py:87
  11.3 1.6 fusion
  12.9 4.4 %all-reduce.9 = bf16[2,64,512]{2,1,0:T(8,128)(2,1)S(1)} all-reduce(f32[2,64,512]{2,1,0:T(8,128)S(1)} %fusion), channel_id=1, replica_groups=mesh['groups'=2,'var'=8,'tm'=2] {'tm'}, use_global_device_ids=true, to_apply=%region_4.0 | all-reduce | flops 65536 | bytes 393216 | tf_op jit(solution)/shard_map/psum | solution.py:96
  18.0 32.3 %all_gather.12 = bf16[2,512,128]{2,1,0:T(8,128)(2,1)S(1)} all-gather(bf16[2,64,128]{2,1,0:T(8,128)(2,1)S(1)} %convolution_convert_fusion.4), channel_id=1, replica_groups=mesh['groups'=2,'var'=8,'tm'=2] {'var'}, dimensions={1}, use_global_device_ids=true | all-gather | bytes 294912 | tf_op jit(solution)/shard_map/all_gather | solution.py:102
  50.6 30.9 %all_gather.13 = bf16[2,512,128]{2,1,0:T(8,128)(2,1)S(1)} all-gather(bf16[2,64,128]{2,1,0:T(8,128)(2,1)S(1)} %convolution_convert_fusion.2), channel_id=1, replica_groups=mesh['groups'=2,'var'=8,'tm'=2] {'var'}, dimensions={1}, use_global_device_ids=true | all-gather | bytes 294912 | tf_op jit(solution)/shard_map/all_gather | solution.py:101
  84.1 0.8 convolution_convert_fusion.1
  85.0 18.8 %all-reduce.6.cloned.1.call-done = bf16[2,64,512]{2,1,0:T(8,128)(2,1)} async-done(((bf16[2,64,512]{2,1,0:T(8,128)(2,1)}), bf16[2,64,512]{2,1,0:T(8,128)(2,1)}) %all-reduce.6.cloned.1.call-update) | async-done | bytes 131088 | tf_op jit(solution)/shard_map/psum | solution.py:106
  103.8 1.1 fusion.36
  104.9 1.1 multiply_reduce_fusion
  106.1 2.1 multiply_convert_fusion.1
  109.1 2.0 all-gather
  111.2 1.0 fusion.31
  112.2 0.8 fusion.34
  113.2 1.6 convolution_bitcast_fusion.1
  115.0 0.9 multiply_reduce_fusion.2
  115.8 1.3 fusion.15
  117.9 0.9 convolution_bitcast_fusion.2
  118.9 2.1 convolution_bitcast_fusion
  121.0 22.7 %psum.62 = f32[512]{0:T(512)} all-reduce(f32[512]{0:T(512)S(1)} %get-tuple-element.7), channel_id=1, replica_groups=mesh['groups'=2,'var'=8,'tm'=2] {'var'}, use_global_device_ids=true, to_apply=%region_18.0 | all-reduce | flops 512 | bytes 4096 | tf_op jit(solution)/shard_map/psum | solution.py:154
  143.7 61.8 %all-reduce.8.cloned.1.call-done = (f32[512,128]{1,0:T(8,128)}, f32[128,512]{1,0:T(8,128)}, f32[512,360]{0,1:T(8,128)}) async-done(((f32[512,128]{1,0:T(8,128)}, f32[128,512]{1,0:T(8,128)}, f32[512,360]{0,1:T(8,128)}), (f32[512,128]{1,0:T(8,128)}, f32[128,512]{1,0:T(8,128)}, f32[512,360]{0,1:T(8,128)})) %all-reduce.8.cloned.1.call-update) | async-done | bytes 1261584 | tf_op jit(solution)/shard_map/psum | solution.py:154
  205.5 1.7 copy.70
  207.2 1.7 copy.71
  208.9 2.0 copy.72
  (82 shorter events, 5.6 us)
Async XLA Ops:
  7.2 4.1 %copy-start = (bf16[2048,512]{1,0:T(8,128)(2,1)S(1)}, bf16[2048,512]{1,0:T(8,128)(2,1)}, u32[]{:S(2)}) copy-start(bf16[2048,512]{1,0:T(8,128)(2,1)} %param.11) | copy-start | bytes 6291460
  7.2 96.6 %all-reduce.6.cloned.1.call-start = ((), (), s32[]{:S(2)}) async-start(), calls=%async_computation | async-start | bytes 262144 | tf_op jit(solution)/shard_map/psum | solution.py:106
  11.2 6.0 %copy-start.10 = (bf16[512,128]{1,0:T(8,128)(2,1)S(1)}, bf16[512,128]{1,0:T(8,128)(2,1)}, u32[]{:S(2)}) copy-start(bf16[512,128]{1,0:T(8,128)(2,1)} %param.13) | copy-start | bytes 393220
  11.2 6.2 %copy-start.11 = (bf16[512,128]{1,0:T(8,128)(2,1)S(1)}, bf16[512,128]{1,0:T(8,128)(2,1)}, u32[]{:S(2)}) copy-start(bf16[512,128]{1,0:T(8,128)(2,1)} %param.12) | copy-start | bytes 393220
  11.3 6.5 %copy-start.12 = (bf16[512,128]{1,0:T(8,128)(2,1)S(1)}, bf16[512,128]{1,0:T(8,128)(2,1)}, u32[]{:S(2)}) copy-start(bf16[512,128]{1,0:T(8,128)(2,1)} %param.14) | copy-start | bytes 393220
  50.3 33.8 %copy-start.2 = (bf16[128,512]{1,0:T(8,128)(2,1)S(1)}, bf16[128,512]{1,0:T(8,128)(2,1)}, u32[]{:S(2)}) copy-start(bf16[128,512]{1,0:T(8,128)(2,1)} %param.15) | copy-start | bytes 393220
  50.4 57.8 %copy-start.6 = (bf16[1,512,128]{1,2,0:T(8,128)(2,1)}, bf16[1,512,128]{1,2,0:T(8,128)(2,1)S(1)}, u32[]{:S(2)}) copy-start(bf16[1,512,128]{1,2,0:T(8,128)(2,1)S(1)} %copy.40) | copy-start | bytes 393220
  50.6 32.3 %copy-start.4 = (bf16[1,512,128]{1,2,0:T(8,128)(2,1)}, bf16[1,512,128]{1,2,0:T(8,128)(2,1)S(1)}, u32[]{:S(2)}) copy-start(bf16[1,512,128]{1,2,0:T(8,128)(2,1)S(1)} %copy.43) | copy-start | bytes 393220
  50.6 55.5 %copy-start.18 = (f32[512]{0:T(512)S(1)}, f32[512]{0:T(512)}, u32[]{:S(2)}) copy-start(f32[512]{0:T(512)} %param.16) | copy-start | bytes 6148
  81.6 22.2 %copy-start.3 = (bf16[1,512,128]{1,2,0:T(8,128)(2,1)}, bf16[1,512,128]{1,2,0:T(8,128)(2,1)S(1)}, u32[]{:S(2)}) copy-start(bf16[1,512,128]{1,2,0:T(8,128)(2,1)S(1)} %copy.41) | copy-start | bytes 393220
  82.0 24.1 %copy-start.20 = (f32[2,64]{1,0:T(2,128)}, f32[2,64]{1,0:T(2,128)S(1)}, u32[]{:S(2)}) copy-start(f32[2,64]{1,0:T(2,128)S(1)} %get-tuple-element.27) | copy-start | bytes 1540
  83.2 22.9 %copy-start.22 = (f32[2,64]{1,0:T(2,128)}, f32[2,64]{1,0:T(2,128)S(1)}, u32[]{:S(2)}) copy-start(f32[2,64]{1,0:T(2,128)S(1)} %get-tuple-element.31) | copy-start | bytes 1540
  84.1 24.1 %copy-start.9 = (bf16[1,64,128]{2,1,0:T(8,128)(2,1)}, bf16[1,64,128]{2,1,0:T(8,128)(2,1)S(1)}, u32[]{:S(2)}) copy-start(bf16[1,64,128]{2,1,0:T(8,128)(2,1)S(1)} %copy.46) | copy-start | bytes 49156
  84.9 120.6 %all-reduce.8.cloned.1.call-start = ((), (), s32[]{:S(2)}) async-start(), calls=%async_computation.1 | async-start | bytes 2523136 | tf_op jit(solution)/shard_map/psum | solution.py:154
  103.8 5.0 %copy-start.7 = (bf16[512,360]{0,1:T(8,128)(2,1)S(1)}, bf16[512,360]{0,1:T(8,128)(2,1)}, u32[]{:S(2)}) copy-start(bf16[512,360]{0,1:T(8,128)(2,1)} %param.17) | copy-start | bytes 1105924
  104.9 6.2 %copy-start.1 = (bf16[2,64,512]{2,1,0:T(8,128)(2,1)S(1)}, bf16[2,64,512]{2,1,0:T(8,128)(2,1)}, u32[]{:S(2)}) copy-start(bf16[2,64,512]{2,1,0:T(8,128)(2,1)} %all-reduce.6.cloned.1.call-done) | copy-start | bytes 393220
  104.9 3.3 %copy-start.14 = (f32[2,64]{1,0:T(2,128)}, f32[2,64]{1,0:T(2,128)S(1)}, u32[]{:S(2)}) copy-start(f32[2,64]{1,0:T(2,128)S(1)} %broadcast_multiply_fusion.2) | copy-start | bytes 1540
  106.1 2.1 copy-start.16
  111.1 6.3 %copy-start.8 = (f32[64,2,64]{0,2,1:T(8,128)S(1)}, f32[64,2,64]{0,2,1:T(8,128)}, u32[]{:S(2)}) copy-start(f32[64,2,64]{0,2,1:T(8,128)} %get-tuple-element.30) | copy-start | bytes 98308
  111.1 6.3 %copy-start.5 = (bf16[1,512,128]{1,2,0:T(8,128)(2,1)S(1)}, bf16[1,512,128]{1,2,0:T(8,128)(2,1)}, u32[]{:S(2)}) copy-start(bf16[1,512,128]{1,2,0:T(8,128)(2,1)} %copy-done.4) | copy-start | bytes 393220
  111.2 6.3 %copy-start.21 = (f32[2,64]{1,0:T(2,128)S(1)}, f32[2,64]{1,0:T(2,128)}, u32[]{:S(2)}) copy-start(f32[2,64]{1,0:T(2,128)} %copy-done.20) | copy-start | bytes 1540
  113.0 5.9 %copy-start.15 = (f32[2,64]{1,0:T(2,128)S(1)}, f32[2,64]{1,0:T(2,128)}, u32[]{:S(2)}) copy-start(f32[2,64]{1,0:T(2,128)} %copy-done.14) | copy-start | bytes 1540
  113.0 5.8 %copy-start.17 = (f32[2,64]{1,0:T(2,128)S(1)}, f32[2,64]{1,0:T(2,128)}, u32[]{:S(2)}) copy-start(f32[2,64]{1,0:T(2,128)} %copy-done.16) | copy-start | bytes 1540
  113.0 5.8 %copy-start.19 = (f32[512]{0:T(512)S(1)}, f32[512]{0:T(512)}, u32[]{:S(2)}) copy-start(f32[512]{0:T(512)} %param.16) | copy-start | bytes 6148
  (1 other events, 0.6 us)
Sparse Core Ops, SparseCore 0:
  85.1 18.7 all-reduce.5
  121.1 84.3 all-reduce.7
